TPU v7x, 32 devices: a whole 2x2x4 slice. The times are simulated.
32 devices in a mesh: au: 4 (over y, x), vert: 8 (over z, core).
Axes of the slice: x: 2, y: 2, z: 4, core: 2. Of those that a mesh axis runs over, the one named last changes fastest.
Arguments:
- visibilities: bfloat16 [768, 2, 2048], P(('au', 'vert')), may hold values from -6 to 6
- baseline_offsets: float32 [768, 2, 128], P(('au', 'vert')), may hold values from -8 to 8
- channel_scale: float32 [16], replicated, may hold values from 0.8 to 1.25
- screen_depth: float32 [768], P(('au', 'vert')), may hold values from -300 to 300
- stations: int32 [768, 2], P(('au', 'vert')), may hold values from 0 to 511
- corners: int32 [768, 2], P(('au', 'vert')), may hold values from 0 to 8191, as said below
- beam_terms: bfloat16 [512, 2, 1024], P(('au', 'vert')), may hold values from -5 to 5
Outputs:
- gridded: float32 [8192, 2, 8192], P('au', None, 'vert')
- dirty_image: float32 [8192, 2, 8192], P(('au', 'vert'))
Inputs may be any that keep to these rules, and one draw needn't show every extreme that they name: Subgrid s belongs to block d = floor(s / 24); with d = r * 8 + c, corners[s, 0] lies in [r * 2048, (r + 1) * 2048) and the columns corners[s, 1] to corners[s, 1] + 31 lie inside one column tile of 1024 columns. At most 6 subgrids of one block lie in one column tile; for every r one column tile holds exactly 6 subgrids of every block of that r.
All inputs are finite; a program needn't handle non-finite values.
Results may differ from a plain program's by a relative error of at most 0.039.
Values may be sent and summed in bfloat16 or wider, within the bound.
No kernel may reach another device: no remote copies, remote signals or barrier semaphores. Data moves between devices by JAX's collectives and lax.ppermute only.
A program may use at most 128 MiB of HBM per device.

v0:
```python
import math

import jax
import jax.numpy as jnp
from jax import lax
from jax.sharding import PartitionSpec as P

G = 8192
SUB = 32


field_view = 0.1
highest = lax.Precision.HIGHEST


def passed_along(value, axis, steps):
    count = lax.axis_size(axis)
    pairs = [(source, (source + steps) % count) for source in range(count)]
    return lax.ppermute(value, axis, pairs)


def complex_einsum(formula, left_operand_pair, right_pair):
    left_re, left_im = left_operand_pair
    right_re, right_im = right_pair
    real_part = jnp.einsum(formula, left_re, right_re, precision=highest) - jnp.einsum(
        formula, left_im, right_im, precision=highest
    )
    imag_part = jnp.einsum(formula, left_re, right_im, precision=highest) + jnp.einsum(
        formula, left_im, right_re, precision=highest
    )
    return (real_part, imag_part)


def complex_product(left_operand_pair, right_pair):
    return (
        left_operand_pair[0] * right_pair[0] - left_operand_pair[1] * right_pair[1],
        left_operand_pair[0] * right_pair[1] + left_operand_pair[1] * right_pair[0],
    )


def unit_table(row_count, col_count, period):
    product = (
        jnp.arange(row_count, dtype=jnp.int32)[:, None]
        * jnp.arange(col_count, dtype=jnp.int32)[None, :]
        % period
    )
    angle = 2.0 * math.pi / period * product.astype(jnp.float32)
    return (jnp.cos(angle), jnp.sin(angle))


def subgrid_table():
    centred = jnp.arange(SUB, dtype=jnp.int32) - SUB // 2
    product = centred[:, None] * centred[None, :] % SUB
    angle = -2.0 * math.pi / SUB * product.astype(jnp.float32)
    return (jnp.cos(angle) / SUB, jnp.sin(angle) / SUB)


def grid_subgrids(vis_items, offset_items, depth_items, beam_first, beam_second, channel_scale):
    item_count = vis_items.shape[0]
    vis_count = vis_items.shape[2]
    pixel_pos = jnp.arange(SUB, dtype=jnp.float32) - SUB // 2
    shift_u = (offset_items[:, 0, :, None] * channel_scale[None, None, :]).reshape(
        item_count, vis_count
    )
    shift_v = (offset_items[:, 1, :, None] * channel_scale[None, None, :]).reshape(
        item_count, vis_count
    )
    angle_u = 2.0 * math.pi / SUB * pixel_pos[None, :, None] * shift_u[:, None, :]
    angle_v = 2.0 * math.pi / SUB * pixel_pos[None, :, None] * shift_v[:, None, :]
    vis_re = vis_items[:, 0, None, :].astype(jnp.float32)
    vis_im = vis_items[:, 1, None, :].astype(jnp.float32)
    cos_u = jnp.cos(angle_u)
    sin_u = jnp.sin(angle_u)
    weighted_re = (vis_re * cos_u - vis_im * sin_u).astype(jnp.bfloat16)
    weighted_im = (vis_re * sin_u + vis_im * cos_u).astype(jnp.bfloat16)
    phasor_re = jnp.cos(angle_v).astype(jnp.bfloat16)
    phasor_im = jnp.sin(angle_v).astype(jnp.bfloat16)
    stacked_left = jnp.concatenate([weighted_re, weighted_im], axis=2)
    stacked_right = jnp.concatenate(
        [
            jnp.concatenate([phasor_re, -phasor_im], axis=2),
            jnp.concatenate([phasor_im, phasor_re], axis=2),
        ],
        axis=1,
    )
    sky_both = jnp.einsum(
        "npk,nqk->npq", stacked_left, stacked_right, preferred_element_type=jnp.float32
    )
    sky_pair = (sky_both[:, :, :SUB], sky_both[:, :, SUB:])
    taper_line = 1.0 - ((2.0 * jnp.arange(SUB, dtype=jnp.float32) + 1.0 - SUB) / SUB) ** 2
    taper_grid = taper_line[:, None] * taper_line[None, :] / math.sqrt(vis_count)
    sky_angle = pixel_pos * field_view / SUB
    radius_sq = sky_angle[:, None] ** 2 + sky_angle[None, :] ** 2
    screen_angle = -math.pi * depth_items[:, None, None] * radius_sq[None, :, :]
    first_beam = beam_first.astype(jnp.float32).reshape(item_count, 2, SUB, SUB)
    second_beam = beam_second.astype(jnp.float32).reshape(item_count, 2, SUB, SUB)
    pair_term = complex_product(
        (first_beam[:, 0], first_beam[:, 1]), (second_beam[:, 0], -second_beam[:, 1])
    )
    mixed = complex_product(sky_pair, pair_term)
    screened = complex_product(mixed, (jnp.cos(screen_angle), jnp.sin(screen_angle)))
    corrected = (screened[0] * taper_grid, screened[1] * taper_grid)
    dft_pair = subgrid_table()
    partial_pair = complex_einsum("ip,npq->niq", dft_pair, corrected)
    uv_pair = complex_einsum("niq,jq->nij", partial_pair, dft_pair)
    return jnp.stack(uv_pair, axis=1).reshape(item_count, 2 * SUB * SUB)


def grid_in_blocks(vis_items, offset_items, depth_items, first_items, second_items, channel_scale):
    item_count = vis_items.shape[0]
    block_size = math.gcd(item_count, 4)
    block_count = item_count // block_size

    def regroup(source):
        return source.reshape((block_count, block_size) + source.shape[1:])

    def grid_block(pieces):
        return grid_subgrids(
            pieces[0], pieces[1], pieces[2], pieces[3], pieces[4], channel_scale
        ).astype(jnp.bfloat16)

    gridded_blocks = lax.map(
        grid_block,
        (
            regroup(vis_items),
            regroup(offset_items),
            regroup(depth_items),
            regroup(first_items),
            regroup(second_items),
        ),
    )
    return gridded_blocks.reshape(item_count, 2 * SUB * SUB)


def add_subgrids(uv_items, offset_items, tile_rows, tile_cols):
    item_count = uv_items.shape[0]
    pieces = uv_items.reshape(item_count, 2, SUB, SUB)
    span_index = jnp.arange(SUB, dtype=jnp.int32)
    column_index = jnp.arange(tile_cols, dtype=jnp.int32)
    column_onehot = (
        column_index[None, None, :] == offset_items[:, 1, None, None] + span_index[None, :, None]
    ).astype(jnp.bfloat16)
    placed = jnp.einsum("mcij,mjv->micv", pieces, column_onehot, preferred_element_type=jnp.float32)
    row_ids = (offset_items[:, 0, None] + span_index[None, :]).reshape(-1)
    return jax.ops.segment_sum(
        placed.reshape(item_count * SUB, 2 * tile_cols), row_ids, num_segments=tile_rows + SUB
    )


def on_device(
    visibilities, baseline_offsets, channel_scale, screen_depth, stations, corners, beam_terms
):
    au_count = lax.axis_size("au")
    vertical_count = lax.axis_size("vert")
    device_count = au_count * vertical_count
    tile_rows = G // au_count
    tile_cols = G // vertical_count
    own_count = visibilities.shape[0]
    capacity = max(2, (2 * own_count + vertical_count - 1) // vertical_count)
    slot_count = vertical_count * capacity
    beam_table = lax.all_gather(beam_terms, ("au", "vert"), axis=0, tiled=True)
    target = corners[:, 1] // tile_cols
    row_offset = corners[:, 0] - lax.axis_index("au") * tile_rows
    col_offset = corners[:, 1] - target * tile_cols
    offsets = jnp.stack([row_offset, col_offset], axis=1)
    chosen = (target[:, None] == jnp.arange(vertical_count, dtype=jnp.int32)[None, :]).astype(
        jnp.int32
    )
    order_index = jnp.arange(own_count, dtype=jnp.int32)
    earlier_mask = (order_index[None, :] < order_index[:, None]).astype(jnp.int32)
    earlier_count = jnp.dot(earlier_mask, chosen)
    slot_rank = jnp.sum(chosen * earlier_count, axis=1)
    slot_index = target * capacity + slot_rank
    placement = jnp.arange(slot_count, dtype=jnp.int32)[:, None] == slot_index[None, :]
    place_whole = placement.astype(jnp.int32)
    uv_items = grid_in_blocks(
        visibilities,
        baseline_offsets,
        screen_depth,
        jnp.take(beam_table, stations[:, 0], axis=0),
        jnp.take(beam_table, stations[:, 1], axis=0),
        channel_scale,
    )
    uv_send = (
        jnp.dot(placement.astype(jnp.bfloat16), uv_items, preferred_element_type=jnp.float32)
        .astype(jnp.bfloat16)
        .reshape(vertical_count, capacity, -1)
    )
    offset_send = jnp.dot(place_whole, offsets).reshape(vertical_count, capacity, 2)
    uv_slots, offset_slots = (
        lax.all_to_all(uv_send, "vert", split_axis=0, concat_axis=0, tiled=True),
        lax.all_to_all(offset_send, "vert", split_axis=0, concat_axis=0, tiled=True),
    )
    extended = add_subgrids(
        uv_slots.reshape(slot_count, 2 * SUB * SUB),
        offset_slots.reshape(slot_count, 2),
        tile_rows,
        tile_cols,
    )
    carried = passed_along(extended[tile_rows:].astype(jnp.bfloat16), "au", 1).astype(jnp.float32)
    uv_tile = extended[:tile_rows].at[:SUB].add(carried).reshape(tile_rows, 2, tile_cols)
    block_rows = G // device_count
    row_blocks = lax.all_to_all(
        uv_tile.astype(jnp.bfloat16), "vert", split_axis=0, concat_axis=2, tiled=True
    ).astype(uv_tile.dtype)
    split_rows = row_blocks.reshape(block_rows, 2, block_rows, device_count)
    short_table = unit_table(block_rows, block_rows, block_rows)
    long_table = unit_table(device_count, device_count, device_count)
    twist_cols = unit_table(block_rows, device_count, G)
    first_pass = complex_einsum("urj,kr->ukj", (split_rows[:, 0], split_rows[:, 1]), short_table)
    first_pass = complex_product(first_pass, (twist_cols[0][None], twist_cols[1][None]))
    second_pass = complex_einsum("ukj,pj->pku", first_pass, long_table)
    spectra = jnp.stack(second_pass, axis=1).reshape(
        au_count, vertical_count, 2, block_rows * block_rows
    )
    arrived = lax.all_to_all(
        lax.all_to_all(spectra.astype(jnp.bfloat16), "au", split_axis=0, concat_axis=0, tiled=True),
        "vert",
        split_axis=1,
        concat_axis=1,
        tiled=True,
    ).astype(spectra.dtype)
    whole_rows = arrived.reshape(device_count, 2, block_rows, block_rows)
    third_pass = complex_einsum("jkl,qj->qkl", (whole_rows[:, 0], whole_rows[:, 1]), long_table)
    twist_rows = unit_table(device_count, block_rows, G)
    third_pass = complex_product(third_pass, (twist_rows[0][:, None, :], twist_rows[1][:, None, :]))
    fourth_pass = complex_einsum("qkl,pl->kpq", third_pass, short_table)
    image_scale = 1.0 / (SUB * math.sqrt(own_count * device_count))
    dirty_image = jnp.stack(fourth_pass, axis=1).reshape(block_rows, 2, G) * image_scale
    return (uv_tile, dirty_image)


def solution(mesh):
    return jax.shard_map(
        on_device,
        mesh=mesh,
        in_specs=(
            P(("au", "vert"), None, None),
            P(("au", "vert"), None, None),
            P(),
            P(("au", "vert")),
            P(("au", "vert"), None),
            P(("au", "vert"), None),
            P(("au", "vert"), None, None),
        ),
        out_specs=(P("au", None, "vert"), P(("au", "vert"), None, None)),
        check_vma=False,
    )
```

profile of v0, /device:TPU:0, one launch (start us, length us, event | category | flops | bytes accessed | tf_op | source)
XLA Modules:
  0.0 1204.2 jit_solution(15473442101179463308)
XLA Ops:
  10.3 6.3 all-to-all-start
  18.2 4.1 all-to-all-done
  22.4 47.8 %all-gather.2.cloned.1.call-done = bf16[512,2,1024]{2,1,0:T(2,128)(2,1)} async-done(((bf16[16,2,1024]{2,1,0:T(2,128)(2,1)}), bf16[512,2,1024]{2,1,0:T(2,128)(2,1)}) %all-gather.2.cloned.1.call-update) | async-done | bytes 2097168 | tf_op jit(solution)/shard_map/all_gather | solution.py:161
  75.2 119.9 %while.15 = (s32[]{:T(128)}, bf16[6,4,2048]{2,1,0:T(4,128)(2,1)S(1)}, bf16[6,4,2,2048]{3,2,1,0:T(2,128)(2,1)}, f32[6,4,2,128]{3,2,1,0:T(2,128)}, f32[16]{0:T(128...) while((s32[]{:T(128)}, ...), condition=%wide.region_2.4_spmd, body=%wide.region_1.3_spmd.sunk | while | flops 94977376 | bytes 7133457 | solution.py:122
  78.1 8.0 fusion.364
  86.1 3.6 fusion.365
  98.1 8.0 fusion.364
  106.1 3.6 fusion.365
  118.1 8.0 fusion.364
  138.0 8.0 fusion.364
  158.0 8.0 fusion.364
  178.0 8.0 fusion.364
  196.1 3.8 all-to-all-start.1
  200.1 9.5 all-to-all-done.1
  212.0 10.1 copy.178
  222.1 15.6 %copy.223 = f32[192,8,2,1024]{3,1,2,0:T(8,128)} copy(f32[192,8,2,1024]{3,2,1,0:T(2,128)} %bitcast.261) | data formatting | bytes 25165824
  237.7 28.3 %scatter_custom_fusion = f32[2080,2048]{1,0:T(8,128)} fusion(s32[1536]{0:T(1024)S(1)} %reshape.493, f32[1536,2048]{1,0:T(8,128)} %bitcast.268, f32[]{:T(128)} %constant.248.clone.1), kind=kCustom, calls=%fused_computation.158 | custom fusion | flops 3145728 | bytes 17039872 | tf_op jit(solution)/shard_map/scatter-add | solution.py:145
  268.5 11.8 slice.178
  281.9 17.6 %copy.179 = f32[2048,2048]{0,1:T(8,128)} copy(f32[2048,2048]{1,0:T(8,128)} %fusion.158) | data formatting | bytes 33554432 | tf_op jit(solution)/shard_map/scatter-add | solution.py:201
  299.6 9.1 convert_element_type.204
  308.6 21.3 %copy.180 = bf16[2048,2,1024]{2,1,0:T(2,128)(2,1)} copy(bf16[2048,2,1024]{0,2,1:T(8,128)(2,1)} %convert_element_type.204) | data formatting | bytes 16777216 | tf_op jit(solution)/shard_map/convert_element_type | solution.py:204
  330.0 5.1 all-to-all-start.2
  335.9 183.1 %all-to-all-done.2 = bf16[2048,2,1024]{2,1,0:T(2,128)(2,1)} async-done(((bf16[2048,2,1024]{2,1,0:T(2,128)(2,1)}), bf16[2048,2,1024]{2,1,0:T(2,128)(2,1)}, u32[]{:S(2)}, u32[]{:S(2)}) %all-to-all-start.2) | async-done | bytes 8388640 | tf_op jit(solution)/shard_map/all_to_all | solution.py:203
  519.0 9.4 copy.181
  528.4 11.6 copy.182
  540.0 6.0 fusion.295
  546.0 7.5 copy.220
  553.5 13.5 %fusion.137 = f32[256,256,32]{1,0,2:T(8,128)} fusion(bf16[256,1,256,32]{2,0,3,1:T(8,128)(2,1)} %copy.220), kind=kOutput, calls=%fused_computation.185 | convolution fusion | flops 6443368448 | bytes 12582912 | tf_op jit(solution)/shard_map/urj,kr->ukj/dot_general | solution.py:28
  567.1 7.8 fusion.139
  574.8 7.5 copy.219
  582.4 7.9 fusion.141
  590.3 21.8 %add_bitcast_fusion.1 = (f32[256,256,32]{0,1,2:T(8,128)}, f32[256,256,32]{0,1,2:T(8,128)}) fusion(f32[256,32]{0,1:T(8,128)S(1)} %get-tuple-element.287, f32[256,32]{0,1:T(8,128)} %get-tuple-element.288, f32[256,256,32]{1,0,2:T(8,128)S(1)} %fusion.141, f32[256,256,32]{1,0,2:T(8,128)} %fusion.137, f32[256,256,32]{1,0,2:T(8,128)S(1)} %copy-done.4, ...), kind=kOutput, calls=%fused_computation.167 | convolution fusion | flops 6460145664 | bytes 46202880 | tf_op jit(solution)/shard_map/urj,kr->ukj/dot_general | solution.py:25
  612.1 10.3 copy.185
  622.4 11.9 fusion.204
  634.3 9.9 fusion.198
  644.2 10.3 copy.186
  654.5 13.0 %fusion.135 = bf16[32,256,256]{1,0,2:T(8,128)(2,1)} fusion(f32[32,256,256]{2,0,1:T(8,128)} %fusion.204, f32[256,256,32]{1,2,0:T(8,128)} %copy.186), kind=kOutput, calls=%fused_computation.181 | convolution fusion | flops 809515008 | bytes 20971520 | tf_op jit(solution)/shard_map/ukj,pj->pku/dot_general | solution.py:25
  667.5 7.5 copy.187
  675.0 5.6 stack.54
  680.7 13.1 %fusion.136 = bf16[32,256,256]{1,0,2:T(8,128)(2,1)} fusion(f32[32,256,256]{2,0,1:T(8,128)} %fusion.198, f32[256,256,32]{1,2,0:T(8,128)} %copy.186), kind=kOutput, calls=%fused_computation.182 | convolution fusion | flops 809515008 | bytes 20971520 | tf_op jit(solution)/shard_map/ukj,pj->pku/dot_general | solution.py:28
  693.8 7.5 copy.190
  701.3 5.6 stack.55
  706.9 7.6 pad_maximum_fusion.1
  714.5 7.3 copy.191
  721.8 97.0 %all_to_all.35 = bf16[4,8,2,65536]{3,1,2,0:T(8,128)(2,1)S(1)} all-to-all(bf16[4,8,2,65536]{3,1,2,0:T(8,128)(2,1)} %copy.191), channel_id=1, replica_groups=mesh['au'=4,'vert'=8] {'au'}, dimensions={0} | all-to-all | bytes 16777216 | tf_op jit(solution)/shard_map/all_to_all | solution.py:217
  818.8 13.0 %copy.192 = bf16[4,8,2,65536]{3,0,2,1:T(4,128)(2,1)} copy(bf16[4,8,2,65536]{3,1,2,0:T(8,128)(2,1)S(1)} %all_to_all.35) | data formatting | bytes 16777216 | tf_op jit(solution)/shard_map/all_to_all | solution.py:217
  831.8 5.2 all-to-all-start.4
  837.1 25.3 %copy.202 = f32[2048,2,1024]{2,1,0:T(2,128)} copy(f32[2048,2,1024]{0,2,1:T(8,128)} %bitcast.258) | data formatting | bytes 33554432
  862.4 158.4 %all-to-all-done.4 = bf16[4,8,2,65536]{3,0,2,1:T(4,128)(2,1)} async-done(((bf16[4,8,2,65536]{3,0,2,1:T(4,128)(2,1)}), bf16[4,8,2,65536]{3,0,2,1:T(4,128)(2,1)}, u32[]{:S(2)}, u32[]{:S(2)}) %all-to-all-start.4) | async-done | bytes 8388640 | tf_op jit(solution)/shard_map/all_to_all | solution.py:216
  1020.9 11.4 copy.193
  1032.2 8.9 copy.224
  1041.1 3.8 fusion.294
  1044.9 6.9 fusion.147
  1051.8 7.1 fusion.148
  1058.9 6.9 fusion.146
  1065.8 15.1 %multiply_subtract_fusion.2 = (f32[32,256,256]{2,0,1:T(8,128)}, f32[32,256,256]{2,0,1:T(8,128)}) fusion(f32[32,256]{1,0:T(8,128)S(1)} %get-tuple-element.289, f32[32,256]{1,0:T(8,128)S(1)} %get-tuple-element.290, f32[32,256,256]{2,0,1:T(8,128)} %fusion.147, f32[32,256,256]{2,0,1:T(8,128)} %fusion.146, f32[32,256,256]{2,0,1:T(8,128)} %fusion.148, ...), kind=kOutput, calls=%fused_computation.164 | convolution fusion | flops 822097920 | bytes 46202880 | tf_op jit(solution)/shard_map/jkl,qj->qkl/dot_general | solution.py:28
  1080.9 19.3 %fusion.123 = f32[256,32,256]{2,0,1:T(8,128)} fusion(f32[32,256,256]{2,0,1:T(8,128)} %get-tuple-element.273), kind=kOutput, calls=%fused_computation.171 | convolution fusion | flops 6443368448 | bytes 16777216 | tf_op jit(solution)/shard_map/qkl,pl->kpq/dot_general | solution.py:25
  1100.3 13.5 %fusion.121 = f32[256,32,256]{2,0,1:T(8,128)S(1)} fusion(f32[32,256,256]{2,0,1:T(8,128)S(1)} %copy-done.1), kind=kOutput, calls=%fused_computation.169 | convolution fusion | flops 6443368448 | bytes 16777216 | tf_op jit(solution)/shard_map/qkl,pl->kpq/dot_general | solution.py:28
  1113.8 17.1 %subtract_bitcast_fusion = f32[256,256,32]{0,1,2:T(8,128)} fusion(f32[256,32,256]{2,0,1:T(8,128)} %fusion.123, f32[32,256,256]{2,0,1:T(8,128)S(1)} %bitcast.260), kind=kOutput, calls=%fused_computation.162 | convolution fusion | flops 6445465600 | bytes 25165824 | tf_op jit(solution)/shard_map/qkl,pl->kpq/dot_general | solution.py:25
  1130.8 11.5 copy.198
  1142.4 14.9 %add_bitcast_fusion = f32[256,256,32]{0,1,2:T(8,128)} fusion(f32[256,32,256]{2,0,1:T(8,128)S(1)} %fusion.121, f32[32,256,256]{2,0,1:T(8,128)S(1)} %bitcast.260), kind=kOutput, calls=%fused_computation.161 | convolution fusion | flops 6445465600 | bytes 25165824 | tf_op jit(solution)/shard_map/qkl,pl->kpq/dot_general | solution.py:28
  1157.3 8.4 copy.201
  1165.7 6.1 maximum_multiply_fusion
  1171.9 25.3 %copy.203 = f32[256,2,8192]{2,1,0:T(2,128)} copy(f32[256,2,8192]{0,2,1:T(8,128)} %maximum_multiply_fusion) | data formatting | bytes 33554432
  (288 shorter events, 81.9 us)
Async XLA Ops:
  7.2 63.0 %all-gather.2.cloned.1.call-start = ((), (), s32[]{:S(2)}) async-start(), calls=%async_computation.5 | async-start | bytes 2162688 | tf_op jit(solution)/shard_map/all_gather | solution.py:161
  10.3 11.9 all-to-all-start
  196.1 13.5 %all-to-all-start.1 = ((bf16[8,6,2048]{2,1,0:T(8,128)(2,1)}), bf16[8,6,2048]{2,1,0:T(8,128)(2,1)S(1)}, u32[]{:S(2)}, u32[]{:S(2)}) async-start(bf16[8,6,2048]{2,1,0:T(8,128)(2,1)} %reshape.466), calls=%async_computation.1 | async-start | bytes 524288 | tf_op jit(solution)/shard_map/all_to_all | solution.py:191
  267.0 13.3 %collective-permute-start = (bf16[32,2048]{1,0:T(8,128)(2,1)S(1)}, bf16[32,2048]{1,0:T(8,128)(2,1)S(1)}, u32[]{:S(2)}, u32[]{:S(2)}) collective-permute-start(bf16[32,2048]{1,0:T(8,128)(2,1)S(1)} %slice.220), channel_id=1, source_target_pairs={{0,8},{8,16},{16,24},{24,0},{1,9},{9,17},{17,25},{25,1},{2,10},{10... | collective-permute-start | bytes 393224 | tf_op jit(solution)/shard_map/ppermute | solution.py:19
  330.0 189.0 %all-to-all-start.2 = ((bf16[2048,2,1024]{2,1,0:T(2,128)(2,1)}), bf16[2048,2,1024]{2,1,0:T(2,128)(2,1)}, u32[]{:S(2)}, u32[]{:S(2)}) async-start(bf16[2048,2,1024]{2,1,0:T(2,128)(2,1)} %copy.180), calls=%async_computation.2 | async-start | bytes 16777216 | tf_op jit(solution)/shard_map/all_to_all | solution.py:203
  553.5 13.5 %copy-start.2 = (bf16[256,1,256,32]{2,0,3,1:T(8,128)(2,1)S(1)}, bf16[256,1,256,32]{2,0,3,1:T(8,128)(2,1)}, u32[]{:S(2)}) copy-start(bf16[256,1,256,32]{2,0,3,1:T(8,128)(2,1)} %copy.220) | copy-start | bytes 12582916
  582.4 7.9 copy-start.3
  582.4 7.9 copy-start.4
  622.4 11.9 copy-start
  831.8 189.1 %all-to-all-start.4 = ((bf16[4,8,2,65536]{3,0,2,1:T(4,128)(2,1)}), bf16[4,8,2,65536]{3,0,2,1:T(4,128)(2,1)}, u32[]{:S(2)}, u32[]{:S(2)}) async-start(bf16[4,8,2,65536]{3,0,2,1:T(4,128)(2,1)} %copy.192), calls=%async_computation.4 | async-start | bytes 16777216 | tf_op jit(solution)/shard_map/all_to_all | solution.py:216
  1080.9 19.3 %copy-start.1 = (f32[32,256,256]{2,0,1:T(8,128)S(1)}, f32[32,256,256]{2,0,1:T(8,128)}, u32[]{:S(2)}) copy-start(f32[32,256,256]{2,0,1:T(8,128)} %get-tuple-element.273) | copy-start | bytes 25165828
  1080.9 32.8 %slice-start = ((s8[8388608]{0:T(1024)(128)(4,1)}), s8[4194304]{0:T(1024)(128)(4,1)S(1)}, s32[]{:S(2)}) async-start(s8[8388608]{0:T(1024)(128)(4,1)} %bitcast.259), calls=%async_computation.6 | async-start | bytes 8388608
  1100.2 13.5 %slice-start.1 = ((s8[8388608]{0:T(1024)(128)(4,1)}), s8[4194304]{0:T(1024)(128)(4,1)S(1)}, s32[]{:S(2)}) async-start(s8[8388608]{0:T(1024)(128)(4,1)} %bitcast.259), calls=%async_computation.7 | async-start | bytes 8388608
  1157.3 8.4 copy-start.5
Sparse Core Ops, SparseCore 0:
  11.0 59.1 all-gather.1
where the time goes:
time: 1220 us; the launch traced here: 1200 us
  waiting for transfers between devices  404 us (33%)
  local copies, waits for them, and re-layouts  308 us (25%)
  matrix products  230 us (19%)
  other arithmetic  128 us (10%)
  blocking collectives  97 us (8%)
  starting transfers between devices  21.9 us (2%)
  between operations  14.5 us (1%)
    all_to_all x1, waiting for transfers between devices, on_device(): lax.all_to_all(uv_tile.astype(jnp.bfloat16), 'vert', split_axis=0, concat...  183 us
    all_to_all x1, waiting for transfers between devices, on_device(): lax.all_to_all(lax.all_to_all(spectra.astype(jnp.bfloat16), 'au', split_a...  158 us
    all_to_all x1, blocking collectives, on_device(): lax.all_to_all(spectra.astype(jnp.bfloat16), 'au', split_axis=0, concat_a...  97 us
    unnamed x22, local copies, waits for them, and re-layouts  90.1 us
    dot_general x16, matrix products, complex_einsum(): jnp.einsum(formula, left_re, right_re, precision=highest)  63.3 us
    dot_general x16, matrix products, complex_einsum(): jnp.einsum(formula, left_re, right_im, precision=highest)  53.6 us
    dot_general x16, matrix products, complex_einsum(): jnp.einsum(formula, left_im, right_im, precision=highest)  52.9 us
    dot_general x16, matrix products, complex_einsum(): jnp.einsum(formula, left_im, right_re, precision=highest)  52.8 us
  transfers between devices with their start and end apart: 6, of which 5 were waited for; matrix products, arithmetic and copies ran while one was open for 4% of the time, Pallas kernels for 0%

commit v1 on v0

v1 whole, which is shorter than its diff:
```python
import functools
import math

import jax
import jax.numpy as jnp
from jax import lax
from jax.experimental import pallas as pl
from jax.experimental.pallas import tpu as pltpu
from jax.sharding import PartitionSpec as P

G = 8192
SUB = 32
HALF = SUB // 2
PACK = 4 * SUB
LANES = 128
FINE = G // SUB
CHUNK = 768
field_view = 0.1
bf16 = jnp.bfloat16
f32 = jnp.float32
VMEM_BYTES = 58 * 1024 * 1024


def cmul(a, b):
    return (a[0] * b[0] - a[1] * b[1], a[0] * b[1] + a[1] * b[0])


def conj(a):
    return (a[0], -a[1])


def sky_kernel(vis_ref, trig_ref, factor_ref, out_ref, left_ref, right_ref):
    vis_count = vis_ref.shape[2]
    step = math.gcd(vis_count, 256)
    row = lax.broadcasted_iota(jnp.int32, (8, step), 0)
    bits = [(row >> bit) % 2 == 1 for bit in range(3)]

    def powers(c, s, extra):
        z = (jnp.broadcast_to(c, (8, step)), jnp.broadcast_to(s, (8, step)))
        low = (jnp.where(bits[0], z[0], 1.0), jnp.where(bits[0], z[1], 0.0))
        power = z
        for bit in (1, 2):
            power = (power[0] * power[0] - power[1] * power[1], 2.0 * power[0] * power[1])
            more = cmul(low, power)
            low = (jnp.where(bits[bit], more[0], low[0]), jnp.where(bits[bit], more[1], low[1]))
        eight = (power[0] * power[0] - power[1] * power[1], 2.0 * power[0] * power[1])
        sixteen = (eight[0] * eight[0] - eight[1] * eight[1], 2.0 * eight[0] * eight[1])
        if extra is not None:
            low = cmul(low, extra)
        blocks = [cmul(low, conj(sixteen)), cmul(low, conj(eight)), low, cmul(low, eight)]
        return [
            jnp.concatenate([blocks[2 * h][part], blocks[2 * h + 1][part]], axis=0).astype(bf16)
            for part in range(2)
            for h in range(2)
        ]

    for start in range(0, vis_count, step):
        at = pl.ds(start, step)
        vis = tuple(
            jnp.broadcast_to(vis_ref[0, part : part + 1, at].astype(f32), (8, step))
            for part in range(2)
        )
        for place, piece in enumerate(powers(trig_ref[0, 0:1, at], trig_ref[0, 1:2, at], vis)):
            left_ref[HALF * place : HALF * (place + 1), at] = piece
        for place, piece in enumerate(powers(trig_ref[0, 2:3, at], trig_ref[0, 3:4, at], None)):
            right_ref[HALF * place : HALF * (place + 1), at] = piece
    both = lax.dot_general(
        left_ref[...], right_ref[...], (((1,), (1,)), ((), ())), preferred_element_type=f32
    )
    sky = (
        both[:SUB, :SUB] - both[SUB:, SUB:],
        both[:SUB, SUB:] + both[SUB:, :SUB],
    )
    done = cmul(sky, (factor_ref[0, :, :SUB], factor_ref[0, :, SUB:]))
    out_ref[0] = jnp.concatenate(
        [done[0][:HALF], done[1][:HALF], done[0][HALF:], done[1][HALF:]], axis=1
    )


def sky_sums(visibilities, trig, factor, interpret=False):
    count, _, vis_count = visibilities.shape
    return pl.pallas_call(
        sky_kernel,
        grid=(count,),
        in_specs=[
            pl.BlockSpec((1, 2, vis_count), lambda s: (s, 0, 0)),
            pl.BlockSpec((1, 4, vis_count), lambda s: (s, 0, 0)),
            pl.BlockSpec((1, SUB, 2 * SUB), lambda s: (s, 0, 0)),
        ],
        out_specs=pl.BlockSpec((1, HALF, PACK), lambda s: (s, 0, 0)),
        out_shape=jax.ShapeDtypeStruct((count, HALF, PACK), f32),
        scratch_shapes=[
            pltpu.VMEM((2 * SUB, vis_count), bf16),
            pltpu.VMEM((2 * SUB, vis_count), bf16),
        ],
        compiler_params=pltpu.CompilerParams(vmem_limit_bytes=VMEM_BYTES),
        cost_estimate=pl.CostEstimate(
            flops=count * 2 * 64 * 64 * vis_count, bytes_accessed=count * 40 * vis_count,
            transcendentals=0,
        ),
        name="sky_sums",
        interpret=interpret,
    )(visibilities, trig, factor)


def correct_kernel(stations_ref, table_ref, sky_ref, right_ref, left_ref, out_ref, mid_ref):
    count = sky_ref.shape[0]
    lane = lax.broadcasted_iota(jnp.int32, (HALF, PACK), 1)
    imag = (lane // SUB) % 2 == 1
    sign = jnp.where(imag, 1.0, -1.0)

    def up(x):
        return pltpu.roll(x, SUB, 1)

    def down(x):
        return pltpu.roll(x, PACK - SUB, 1)

    for s in range(count):
        first = table_ref[stations_ref[2 * s]].astype(f32)
        second = table_ref[stations_ref[2 * s + 1]].astype(f32)
        second_up, second_down = up(second), down(second)
        first_swap = jnp.where(imag, up(first), down(first))
        pair = first * jnp.where(imag, second_up, second) - sign * first_swap * jnp.where(
            imag, second, second_down
        )
        pair_up, pair_down = up(pair), down(pair)
        sky = sky_ref[s]
        sky_swap = jnp.where(imag, up(sky), down(sky))
        corrected = sky * jnp.where(imag, pair_up, pair) + sign * sky_swap * jnp.where(
            imag, pair, pair_down
        )
        mid_ref[HALF * s : HALF * (s + 1), :] = corrected.astype(bf16)
    mid = jnp.dot(mid_ref[...], right_ref[...], preferred_element_type=f32).astype(bf16)
    for s in range(count):
        rows = mid[HALF * s : HALF * (s + 1)]
        tall = jnp.concatenate([rows[:, : 2 * SUB], rows[:, 2 * SUB :]], axis=0)
        four = jnp.dot(left_ref[...], tall, preferred_element_type=f32)
        real = four[:SUB, :SUB] - four[SUB:, SUB:]
        image = four[:SUB, SUB:] + four[SUB:, :SUB]
        out_ref[s] = jnp.concatenate(
            [real[:HALF], image[:HALF], real[HALF:], image[HALF:]], axis=1
        ).astype(bf16)


def corrected_subgrids(stations, table, sky, interpret=False):
    count = sky.shape[0]
    centred = jnp.arange(SUB, dtype=jnp.int32) - HALF
    index = jnp.arange(SUB, dtype=jnp.int32)
    angle = 2.0 * math.pi / SUB * (centred[:, None] * centred[None, :] % SUB).astype(f32)
    cols_re, cols_im = jnp.cos(angle) / SUB, -jnp.sin(angle) / SUB
    block = jnp.concatenate(
        [
            jnp.concatenate([cols_re.T, cols_im.T], axis=1),
            jnp.concatenate([-cols_im.T, cols_re.T], axis=1),
        ],
        axis=0,
    )
    right = jnp.kron(jnp.eye(2, dtype=f32), block).astype(bf16)
    angle = 2.0 * math.pi / SUB * ((index - HALF)[:, None] * centred[None, :] % SUB).astype(f32)
    left = jnp.concatenate([jnp.cos(angle) / SUB, -jnp.sin(angle) / SUB], axis=0).astype(bf16)
    return pl.pallas_call(
        correct_kernel,
        grid_spec=pltpu.PrefetchScalarGridSpec(
            num_scalar_prefetch=1,
            grid=(1,),
            in_specs=[
                pl.BlockSpec(table.shape, lambda i, *_: (0, 0, 0)),
                pl.BlockSpec(sky.shape, lambda i, *_: (0, 0, 0)),
                pl.BlockSpec(right.shape, lambda i, *_: (0, 0)),
                pl.BlockSpec(left.shape, lambda i, *_: (0, 0)),
            ],
            out_specs=pl.BlockSpec((count, HALF, PACK), lambda i, *_: (0, 0, 0)),
            scratch_shapes=[pltpu.VMEM((HALF * count, PACK), bf16)],
        ),
        out_shape=jax.ShapeDtypeStruct((count, HALF, PACK), bf16),
        compiler_params=pltpu.CompilerParams(vmem_limit_bytes=VMEM_BYTES),
        name="correct",
        interpret=interpret,
    )(stations.reshape(-1), table, sky, right, left)


def tile_kernel(
    block_ref, place_ref, uv_ref, out_ref, total_ref, sems, *, per_block, tile_rows, tile_cols
):
    del block_ref
    step = pl.program_id(0)
    lanes = 2 * tile_cols // LANES
    rows_all = total_ref.shape[0]
    zero_rows = math.gcd(rows_all, 1024)

    @pl.when(step == 0)
    def _():
        def clear(i, carry):
            total_ref[pl.ds(pl.multiple_of(i * zero_rows, zero_rows), zero_rows), :] = jnp.zeros(
                (zero_rows, LANES), f32
            )
            return carry

        lax.fori_loop(0, rows_all // zero_rows, clear, 0)

    lane = lax.broadcasted_iota(jnp.int32, (8, LANES), 1)
    row = lax.broadcasted_iota(jnp.int32, (8, LANES), 0)

    def one(s, carry):
        first = (step * per_block + s) * 2
        row_at = place_ref[first]
        col_at = place_ref[first + 1]

        @pl.when(jnp.logical_and(row_at >= 0, col_at >= 0))
        def _():
            packed = uv_ref[pl.ds(pl.multiple_of(s * HALF, HALF), HALF), :].astype(f32)
            tile = col_at // LANES
            offset = col_at % LANES
            shift = row_at % SUB
            base = row_at - shift

            def place(over):
                inside = lane < offset + SUB - LANES if over else (lane >= offset) & (lane < offset + SUB)
                for h in range(2):
                    for part in range(2):
                        from_lane = (2 * h + part) * SUB
                        moved = pltpu.roll(packed, lax.rem(offset - from_lane + LANES, LANES), 1)
                        for group in range(2):
                            values = moved[8 * group : 8 * (group + 1)]
                            first_row = HALF * h + 8 * group
                            late = row + first_row >= shift
                            for wrapped in range(2):
                                keep = jnp.logical_and(inside, late if wrapped == 0 else ~late)
                                start = (base + SUB * wrapped + first_row) * lanes
                                start = start + 2 * (tile + over) + part
                                at = pl.ds(start, 8, stride=lanes)
                                total_ref[at, :] = total_ref[at, :] + jnp.where(keep, values, 0.0)

            place(0)

            @pl.when(offset + SUB > LANES)
            def _():
                place(1)

        return carry

    lax.fori_loop(0, per_block, one, 0)

    @pl.when(step == pl.num_programs(0) - 1)
    def _():
        pieces = sems.shape[0]
        size = tile_rows * lanes // pieces
        copies = [
            pltpu.make_async_copy(
                total_ref.at[pl.ds(SUB * lanes + i * size, size), :],
                out_ref.at[pl.ds(i * size, size), :],
                sems.at[i],
            )
            for i in range(pieces)
        ]
        for copy in copies:
            copy.start()
        for copy in copies:
            copy.wait()


def uv_tile(uv_all, corners_all, au_index, vert_index, au_count, vert_count, interpret=False):
    total = uv_all.shape[0]
    tile_rows, tile_cols = G // au_count, G // vert_count
    per_block = total // au_count
    lanes = 2 * tile_cols // LANES
    before = lax.rem(au_index + au_count - 1, au_count)
    blocks = jnp.stack([au_index, before])
    held = corners_all.reshape(au_count, per_block, 2)
    held = jnp.concatenate(
        [lax.dynamic_index_in_dim(held, au_index, 0, False), lax.dynamic_index_in_dim(held, before, 0, False)]
    )
    row_at = (held[:, 0] - au_index * tile_rows + SUB + G) % G
    row_at = jnp.where(row_at < tile_rows + SUB, row_at, -1)
    col_at = held[:, 1] - vert_index * tile_cols
    col_at = jnp.where((col_at >= 0) & (col_at < tile_cols), col_at, -1)
    places = jnp.stack([row_at, col_at], axis=1).reshape(-1)
    rows_all = (tile_rows + 3 * SUB) * lanes
    result = pl.pallas_call(
        functools.partial(
            tile_kernel, per_block=per_block, tile_rows=tile_rows, tile_cols=tile_cols
        ),
        grid_spec=pltpu.PrefetchScalarGridSpec(
            num_scalar_prefetch=2,
            grid=(2,),
            in_specs=[pl.BlockSpec((per_block * HALF, PACK), lambda i, block, place: (block[i], 0))],
            out_specs=pl.BlockSpec(memory_space=pl.ANY),
            scratch_shapes=[pltpu.VMEM((rows_all, LANES), f32), pltpu.SemaphoreType.DMA((4,))],
        ),
        out_shape=jax.ShapeDtypeStruct((tile_rows * lanes, LANES), f32),
        compiler_params=pltpu.CompilerParams(vmem_limit_bytes=VMEM_BYTES),
        name="uv_tile",
        interpret=interpret,
    )(blocks, places, uv_all.reshape(total * HALF, PACK))
    result = result.reshape(tile_rows, tile_cols // LANES, 2, LANES)
    return jnp.transpose(result, (0, 2, 1, 3)).reshape(tile_rows, 2, tile_cols)


def short_transform(values):
    count = len(values)
    if count == 1:
        return values
    even = short_transform(values[0::2])
    odd = short_transform(values[1::2])
    low, high = [], []
    for k in range(count // 2):
        re, im = odd[k]
        if k == 0:
            turned = (re, im)
        elif 4 * k == count:
            turned = (-im, re)
        elif 8 * k == count:
            root = math.sqrt(0.5)
            turned = ((re - im) * root, (re + im) * root)
        elif 8 * k == 3 * count:
            root = math.sqrt(0.5)
            turned = ((re + im) * -root, (re - im) * root)
        else:
            c, s = math.cos(2 * math.pi * k / count), math.sin(2 * math.pi * k / count)
            turned = (re * c - im * s, re * s + im * c)
        low.append((even[k][0] + turned[0], even[k][1] + turned[1]))
        high.append((even[k][0] - turned[0], even[k][1] - turned[1]))
    return low + high


def image_kernel(
    uv_ref, corner_ref, phase_ref, columns_ref, unit_ref, count_ref, twist_ref,
    out_ref, uv_wide, here, after, shifts, total, *, chunks, row_block
):
    step = pl.program_id(0)
    size = uv_ref.shape[0] // HALF
    image_rows = phase_ref.shape[1]

    @pl.when(step < chunks * HALF)
    def _():
        pair = lax.rem(step, HALF)
        chunk = step // HALF

        @pl.when(pair == 0)
        def _():
            uv_wide[...] = uv_ref[...].astype(f32)
            corner = corner_ref[...]
            coarse, shift = corner // SUB, corner % SUB

            def looked_up(index, length, table):
                place = lax.broadcasted_iota(jnp.int32, (length, size), 0)
                one = (place == index).astype(f32).astype(bf16)
                return lax.dot_general(
                    one, table, (((0,), (0,)), ((), ())), preferred_element_type=f32
                )

            here[...] = looked_up(coarse, FINE, unit_ref[...]).astype(bf16)
            after[...] = looked_up(lax.rem(coarse + 1, FINE), FINE, unit_ref[...]).astype(bf16)
            shifts[...] = looked_up(shift, SUB, count_ref[...])

        rows = uv_wide[pl.ds(pair, size, stride=HALF), :].astype(bf16)
        spread = lax.dot_general(
            columns_ref[...], rows, (((1,), (1,)), ((), ())), preferred_element_type=f32
        )
        for h in range(2):
            index = pair + HALF * h
            start = 2 * image_rows * h
            part = (spread[start : start + image_rows], spread[start + image_rows : start + 2 * image_rows])
            turned = cmul(part, (phase_ref[0], phase_ref[1]))
            left = jnp.concatenate([turned[0].astype(bf16), turned[1].astype(bf16)], axis=1)
            late = shifts[:, :1] > index.astype(f32)
            table = jnp.where(late, after[...], here[...])
            right = jnp.concatenate(
                [table, jnp.concatenate([-table[:, FINE:], table[:, :FINE]], axis=1)], axis=0
            )
            sums = jnp.dot(left, right, preferred_element_type=f32)
            twist = twist_ref[pl.ds(index, 1), :]
            done = cmul((sums[:, :FINE], sums[:, FINE:]), (twist[:, :FINE], twist[:, FINE:]))

            if chunks == 1:
                total[index, 0] = done[0]
                total[index, 1] = done[1]
            else:
                @pl.when(chunk == 0)
                def _():
                    total[index, 0] = done[0]
                    total[index, 1] = done[1]

                @pl.when(chunk > 0)
                def _():
                    total[index, 0] += done[0]
                    total[index, 1] += done[1]

    @pl.when(step >= chunks * HALF)
    def _():
        first = (step - chunks * HALF) * row_block
        wide = 2 * G // LANES

        def eight_rows(group, carry):
            at = pl.ds(pl.multiple_of(first + 8 * group, 8), 8)
            for tile in range(FINE // LANES):
                lanes = pl.ds(tile * LANES, LANES)
                values = [(total[n, 0, at, lanes], total[n, 1, at, lanes]) for n in range(SUB)]
                for k, value in enumerate(short_transform(values)):
                    for part in range(2):
                        column = 2 * (k * (FINE // LANES) + tile) + part
                        out_ref[pl.ds(group * 8 * wide + column, 8, stride=wide), :] = value[part]
            return carry

        lax.fori_loop(0, row_block // 8, eight_rows, 0)


def image_rows_of(uv_all, corners_all, first_row, image_rows, interpret=False):
    total = uv_all.shape[0]
    size = math.gcd(total, CHUNK)
    chunks = total // size
    row_block = math.gcd(image_rows, 32)
    outs = image_rows // row_block
    wide = 2 * G // LANES
    rows = first_row + jnp.arange(image_rows, dtype=jnp.int32)
    turn = 2.0 * math.pi / G
    angle = turn * (rows[:, None] * corners_all[None, :, 1] % G).astype(f32)
    phase = jnp.stack([jnp.cos(angle), jnp.sin(angle)])
    angle = turn * (rows[:, None] * jnp.arange(SUB, dtype=jnp.int32)[None, :] % G).astype(f32)
    re, im = jnp.cos(angle), jnp.sin(angle)
    block = jnp.concatenate(
        [jnp.concatenate([re, -im], axis=1), jnp.concatenate([im, re], axis=1)], axis=0
    )
    columns = jnp.kron(jnp.eye(2, dtype=f32), block).astype(bf16)
    fine = jnp.arange(FINE, dtype=jnp.int32)
    angle = 2.0 * math.pi / FINE * (fine[:, None] * fine[None, :] % FINE).astype(f32)
    unit = jnp.concatenate([jnp.cos(angle), jnp.sin(angle)], axis=1).astype(bf16)
    angle = turn * (jnp.arange(SUB, dtype=jnp.int32)[:, None] * fine[None, :]).astype(f32)
    scale = 1.0 / (SUB * math.sqrt(total))
    twist = jnp.concatenate([jnp.cos(angle), jnp.sin(angle)], axis=1) * scale
    counts = jnp.broadcast_to(jnp.arange(SUB, dtype=f32)[:, None], (SUB, LANES)).astype(bf16)
    last = chunks - 1

    def chunk_of(i):
        return jnp.minimum(i // HALF, last)

    result = pl.pallas_call(
        functools.partial(image_kernel, chunks=chunks, row_block=row_block),
        grid=(chunks * HALF + outs,),
        in_specs=[
            pl.BlockSpec((size * HALF, PACK), lambda i: (chunk_of(i), 0)),
            pl.BlockSpec((1, size), lambda i: (0, chunk_of(i))),
            pl.BlockSpec((2, image_rows, size), lambda i: (0, 0, chunk_of(i))),
            pl.BlockSpec(columns.shape, lambda i: (0, 0)),
            pl.BlockSpec(unit.shape, lambda i: (0, 0)),
            pl.BlockSpec(counts.shape, lambda i: (0, 0)),
            pl.BlockSpec(twist.shape, lambda i: (0, 0)),
        ],
        out_specs=pl.BlockSpec(
            (row_block * wide, LANES), lambda i: (jnp.maximum(i - chunks * HALF, 0), 0)
        ),
        out_shape=jax.ShapeDtypeStruct((image_rows * wide, LANES), f32),
        scratch_shapes=[
            pltpu.VMEM((size * HALF, PACK), f32),
            pltpu.VMEM((size, 2 * FINE), bf16),
            pltpu.VMEM((size, 2 * FINE), bf16),
            pltpu.VMEM((size, LANES), f32),
            pltpu.VMEM((SUB, 2, image_rows, FINE), f32),
        ],
        compiler_params=pltpu.CompilerParams(vmem_limit_bytes=VMEM_BYTES),
        name="image",
        interpret=interpret,
    )(
        uv_all.reshape(total * HALF, PACK), corners_all[:, 0].reshape(1, total),
        phase, columns, unit, counts, twist,
    )
    result = result.reshape(image_rows, G // LANES, 2, LANES)
    return jnp.transpose(result, (0, 2, 1, 3)).reshape(image_rows, 2, G)


def packed_beams(beam_terms):
    count = beam_terms.shape[0]
    parts = beam_terms.reshape(count, 2, 2, HALF, SUB)
    return jnp.transpose(parts, (0, 3, 2, 1, 4)).reshape(count, HALF, PACK)


def base_turns(baseline_offsets, channel_scale):
    count, _, times = baseline_offsets.shape
    shifts = (baseline_offsets[:, :, :, None] * channel_scale).reshape(count, 2, -1)
    angle = 2.0 * math.pi / SUB * shifts
    return jnp.stack([jnp.cos(angle), jnp.sin(angle)], axis=2).reshape(count, 4, -1)


def pixel_factor(screen_depth, shift, vis_count):
    pixel = jnp.arange(SUB, dtype=f32) - HALF
    taper_line = 1.0 - ((2.0 * jnp.arange(SUB, dtype=f32) + 1.0 - SUB) / SUB) ** 2
    taper = taper_line[:, None] * taper_line[None, :] / math.sqrt(vis_count)
    sky_angle = pixel * field_view / SUB
    radius_sq = sky_angle[:, None] ** 2 + sky_angle[None, :] ** 2
    turns = shift[:, None] * (jnp.arange(SUB, dtype=jnp.int32) - HALF)[None, :] % SUB
    angle = (
        -math.pi * screen_depth[:, None, None] * radius_sq
        + (2.0 * math.pi / SUB * turns.astype(f32))[:, :, None]
    )
    return jnp.concatenate([jnp.cos(angle) * taper, jnp.sin(angle) * taper], axis=2)


def on_device(
    visibilities, baseline_offsets, channel_scale, screen_depth, stations, corners, beam_terms
):
    au_count = lax.axis_size("au")
    vert_count = lax.axis_size("vert")
    au_index, vert_index = lax.axis_index("au"), lax.axis_index("vert")
    image_rows = G // (au_count * vert_count)
    vis_count = visibilities.shape[2]
    both = ("au", "vert")
    table = lax.all_gather(packed_beams(beam_terms), both, axis=0, tiled=True)
    corners_all = lax.all_gather(corners, both, axis=0, tiled=True)
    factor = pixel_factor(screen_depth, corners[:, 0] % SUB, vis_count)
    sky = sky_sums(visibilities, base_turns(baseline_offsets, channel_scale), factor)
    uv_own = corrected_subgrids(stations, table, sky)
    uv_all = lax.all_gather(uv_own, both, axis=0, tiled=True)
    gridded = uv_tile(uv_all, corners_all, au_index, vert_index, au_count, vert_count)
    first_row = (au_index * vert_count + vert_index) * image_rows
    dirty_image = image_rows_of(uv_all, corners_all, first_row, image_rows)
    return (gridded, dirty_image)


def solution(mesh):
    return jax.shard_map(
        on_device,
        mesh=mesh,
        in_specs=(
            P(("au", "vert"), None, None),
            P(("au", "vert"), None, None),
            P(),
            P(("au", "vert")),
            P(("au", "vert"), None),
            P(("au", "vert"), None),
            P(("au", "vert"), None, None),
        ),
        out_specs=(P("au", None, "vert"), P(("au", "vert"), None, None)),
        check_vma=False,
    )
```

time: 1220 us -> 214 us (0.18); the launches traced: 1200 us -> 210 us
  waiting for transfers between devices: 404 us -> 35.1 us
  local copies, waits for them, and re-layouts: 308 us -> 15.1 us
  matrix products: 230 us -> 0 us
  other arithmetic: 128 us -> 13.8 us
  Pallas kernels: 0 us -> 92.4 us
  blocking collectives: 97 us -> 39.6 us
  starting transfers between devices: 21.9 us -> 0.08 us
    all_to_all x4 -> x0, waiting for transfers between devices: 355 us -> none  [the longest x1 183 us: on_device(): lax.all_to_all(uv_tile.astype(jnp.bfloat16), 'vert', split_axis=0, concat...]
    dot_general x74 -> x0, matrix products: 230 us -> none  [the longest x16 63.3 us: complex_einsum(): jnp.einsum(formula, left_re, right_re, precision=highest)]
    all_to_all x1 -> x0, blocking collectives: 97 us -> none  [on_device(): lax.all_to_all(spectra.astype(jnp.bfloat16), 'au', split_axis=0, concat_a...]
    pallas_call x0 -> x4, Pallas kernels: none -> 92.4 us  [the longest x1 51.9 us: image_rows_of(): pl.pallas_call(functools.partial(image_kernel, chunks=chunks, row_block=r...]
    unnamed x22 -> x19, local copies, waits for them, and re-layouts: 90.1 us -> 2.19 us
    convert_element_type x19 -> x4, other arithmetic: 57 us -> 0.36 us  [the longest x1 0.24 us: image_rows_of(): columns = jnp.kron(jnp.eye(2, dtype=f32), block).astype(bf16)]
    all_to_all x5 -> x0, local copies, waits for them, and re-layouts: 45.4 us -> none  [the longest x2 21 us: on_device(): lax.all_to_all(uv_tile.astype(jnp.bfloat16), 'vert', split_axis=0, concat...]
    all_gather x0 -> x1, blocking collectives: none -> 39.6 us  [on_device(): corners_all = lax.all_gather(corners, both, axis=0, tiled=True)]
  transfers between devices with their start and end apart: 6 -> 2, of which waited for: 5 -> 2; matrix products, arithmetic and copies ran while one was open for 4% -> 12% of each run, Pallas kernels for 0% -> 9%
where the time goes in v1:
time: 214 us; the launch traced here: 210 us
  Pallas kernels  92.4 us (43%)
  blocking collectives  39.6 us (19%)
  waiting for transfers between devices  35.1 us (16%)
  local copies, waits for them, and re-layouts  15.1 us (7%)
  between operations  14.3 us (7%)
  other arithmetic  13.8 us (6%)
    pallas_call x1, Pallas kernels, image_rows_of(): pl.pallas_call(functools.partial(image_kernel, chunks=chunks, row_block=r...  51.9 us
    all_gather x1, blocking collectives, on_device(): corners_all = lax.all_gather(corners, both, axis=0, tiled=True)  39.6 us
    all_gather x1, waiting for transfers between devices, on_device(): table = lax.all_gather(packed_beams(beam_terms), both, axis=0, tiled=True)  27.4 us
    pallas_call x1, Pallas kernels, sky_sums(): pl.pallas_call(sky_kernel, grid=(count,), in_specs=[pl.BlockSpec((1, 2, v...  18.1 us
    pallas_call x1, Pallas kernels, uv_tile(): pl.pallas_call(functools.partial(tile_kernel, per_block=per_block, tile_r...  17.6 us
    all_gather x1, waiting for transfers between devices, on_device(): uv_all = lax.all_gather(uv_own, both, axis=0, tiled=True)  7.7 us
    pallas_call x1, Pallas kernels, corrected_subgrids(): pl.pallas_call(correct_kernel, grid_spec=pltpu.PrefetchScalarGridSpec(num...  4.84 us
  transfers between devices with their start and end apart: 2, of which 2 were waited for; matrix products, arithmetic and copies ran while one was open for 12% of the time, Pallas kernels for 9%

profile of v1, /device:TPU:0, one launch (start us, length us, event | category | flops | bytes accessed | tf_op | source)
XLA Modules:
  0.0 210.5 jit_solution(13027263984499784912)
XLA Ops:
  7.2 0.0 all-gather.4.cloned.1.call-start
  7.2 1.0 reshape.367
  8.3 0.2 copy.51
  8.5 0.8 reshape.368
  9.3 0.0 all-gather.4.cloned.1.call-update
  9.3 0.0 all-gather.6.cloned.1.call-start
  9.4 0.0 copy-start.3
  9.4 0.5 copy-done.3
  9.9 0.1 copy.40
  10.0 0.8 copy.36
  10.8 0.7 reshape.366.stations_ref
  11.5 0.7 copy.38
  12.2 0.0 copy-start.1
  12.2 0.7 fusion.32
  13.0 0.0 copy-done.1
  13.0 0.1 maximum_maximum_fusion.1
  13.1 0.1 multiply_convert_fusion.1
  13.2 0.7 convert_element_type.79.right_ref
  13.9 0.7 mul.399
  14.6 0.1 mul.400
  14.6 0.9 mul.397
  15.5 2.5 %mul.398 = f32[24,2,1,2048]{3,0,1,2:T(8,128)S(1)} reshape(f32[24,2,128,16]{3,2,0,1:T(8,128)S(1)} %mul.397) | data formatting | bytes 786432 | tf_op jit(solution)/shard_map/mul | solution.py:479
  18.0 1.4 fusion.6
  19.4 0.0 copy-start.6
  19.5 0.0 copy-start.5
  19.5 0.0 copy-start.2
  19.5 0.1 pad_maximum_fusion.1
  19.5 0.6 copy.39
  20.2 1.6 reshape.369.trig_ref
  21.7 0.0 copy-done.6
  21.8 0.0 copy-done.5
  21.8 0.0 copy-done.2
  21.8 0.1 fusion.27
  21.9 0.1 multiply_multiply_fusion.1
  21.9 1.5 cosine_multiply_fusion
  23.4 0.9 pad_maximum_fusion.2.factor_ref
  24.4 18.1 %sky_sums.1.sky_ref = f32[24,16,128]{2,1,0:T(8,128)} custom-call(bf16[24,2,2048]{2,1,0:T(2,128)(2,1)} %vis_ref.1, f32[24,4,2048]{2,1,0:T(4,128)} %reshape.369.trig_ref, f32[24,32,64]{2,1,0:T(8,128)} %pad_maximum_fusion.2.factor_ref), custom_call_target="tpu_custom_call" | custom-call | flops 402653184 | bytes 1966080 | tf_op jit(solution)/shard_map/sky_sums/pallas_call | solution.py:82
  42.4 0.0 copy-done
  42.4 0.6 pad_maximum_fusion.4.left_ref
  43.1 27.4 %all-gather.4.cloned.1.call-done.table_ref = bf16[512,16,128]{2,1,0:T(8,128)(2,1)} async-done(((bf16[16,16,128]{2,1,0:T(8,128)(2,1)}), bf16[512,16,128]{2,1,0:T(8,128)(2,1)}) %all-gather.4.cloned.1.call-update) | async-done | bytes 2097168 | tf_op jit(solution)/shard_map/all_gather | solution.py:507
  70.5 4.8 %correct.1 = bf16[24,16,128]{2,1,0:T(8,128)(2,1)} custom-call(s32[48]{0:T(128)} %reshape.366.stations_ref, bf16[512,16,128]{2,1,0:T(8,128)(2,1)} %all-gather.4.cloned.1.call-done.table_ref, f32[24,16,128]{2,1,0:T(8,128)} %sky_sums.1.sky_ref, bf16[128,128]{1,0:T(8,128)(2,1)} %convert_element_type.79.right_ref, bf16[64,32]{1,0:T(8,128)(2,1)} %pad_maximum_fusion.4.left_ref), custom_call_target="tpu_custom_call" | custom-call | tf_op jit(solution)/shard_map/correct/pallas_call | solution.py:161
  75.3 0.0 all-gather.6.cloned.1.call-update
  75.3 39.6 %all-gather = s32[32,24,2]{1,2,0:T(2,128)S(1)} all-gather(s32[1,24,2]{1,2,0:T(2,128)S(1)} %bitcast.45), channel_id=1, replica_groups=mesh['au'=4,'vert'=8] {'au','vert'}, dimensions={0}, use_global_device_ids=true | all-gather | bytes 6336 | tf_op jit(solution)/shard_map/all_gather | solution.py:508
  115.0 0.1 reshape.376
  115.1 0.1 reshape.364
  115.2 0.1 fusion.29
  115.3 0.0 copy-done.4
  115.3 0.2 multiply_convert_fusion
  115.6 0.9 copy.43.columns_ref
  116.5 0.1 compare_select_fusion
  116.6 0.1 copy.35
  116.8 0.7 reshape.365.place_ref
  117.5 0.7 pad_add_fusion.2.block_ref
  118.2 0.1 fusion.16
  118.3 0.6 maximum_multiply_fusion.twist_ref
  118.9 1.1 sine_convert_fusion
  120.0 0.7 pad_maximum_fusion.3.unit_ref
  120.8 0.6 slice_reduce_fusion
  121.4 3.1 %fusion.4 = (f32[1,256,768]{2,1,0:T(8,128)S(1)}, f32[1,256,768]{2,1,0:T(8,128)S(1)}) fusion(s32[768]{0:T(1024)S(1)} %get-tuple-element.8, s32[256]{0:T(256)S(1)} %iota_add_fusion), kind=kLoop, calls=%fused_computation.16 | loop fusion | flops 2752512 | bytes 1576960 | tf_op jit(solution)/shard_map/cos | solution.py:418
  124.5 1.3 pad_maximum_fusion.phase_ref
  125.8 7.7 %all-gather.6.cloned.1.call-done = bf16[768,16,128]{2,1,0:T(8,128)(2,1)} async-done(((bf16[24,16,128]{2,1,0:T(8,128)(2,1)}), bf16[768,16,128]{2,1,0:T(8,128)(2,1)}) %all-gather.6.cloned.1.call-update) | async-done | bytes 3145744 | tf_op jit(solution)/shard_map/all_gather | solution.py:512
  133.5 17.6 %uv_tile.1 = f32[32768,128]{1,0:T(8,128)} custom-call(s32[2]{0:T(128)} %pad_add_fusion.2.block_ref, s32[768]{0:T(1024)} %reshape.365.place_ref, bf16[12288,128]{1,0:T(8,128)(2,1)} %bitcast.40), custom_call_target="tpu_custom_call" | custom-call | tf_op jit(solution)/shard_map/uv_tile/pallas_call | solution.py:279
  151.1 0.7 broadcast_in_dim.11.count_ref
  151.7 51.9 %image.1 = f32[32768,128]{1,0:T(8,128)} custom-call(bf16[12288,128]{1,0:T(8,128)(2,1)} %bitcast.41, s32[1,768]{1,0:T(1,128)} %get-tuple-element.9.corner_ref, f32[2,256,768]{2,1,0:T(8,128)} %pad_maximum_fusion.phase_ref, bf16[1024,128]{1,0:T(8,128)(2,1)} %copy.43.columns_ref, bf16[256,512]{1,0:T(8,128)(2,1)} %pad_maximum_fusion.3.unit_ref, ...), custom_call_target="tpu_custom_call" | custom-call | tf_op jit(solution)/shard_map/image/pallas_call | solution.py:437
  (16 shorter events, 0.1 us)
Async XLA Ops:
  7.2 63.3 %all-gather.4.cloned.1.call-start = ((), (), s32[]{:S(2)}) async-start(), calls=%async_computation | async-start | bytes 2162688 | tf_op jit(solution)/shard_map/all_gather | solution.py:507
  9.3 124.1 %all-gather.6.cloned.1.call-start = ((), (), s32[]{:S(2)}) async-start(), calls=%async_computation.1 | async-start | bytes 3244032 | tf_op jit(solution)/shard_map/all_gather | solution.py:512
  9.4 0.5 copy-start.3
  12.2 0.8 copy-start.1
  19.4 2.3 %copy-start.6 = (f32[24]{0:T(128)S(1)}, f32[24]{0:T(128)}, u32[]{:S(2)}) copy-start(f32[24]{0:T(128)} %param.10) | copy-start | bytes 292
  19.5 2.3 %copy-start.5 = (s32[24,2]{0,1:T(2,128)S(1)}, s32[24,2]{0,1:T(2,128)}, u32[]{:S(2)}) copy-start(s32[24,2]{0,1:T(2,128)} %param.12) | copy-start | bytes 580
  19.5 2.3 %copy-start.2 = (s32[32]{0:T(128)S(1)}, s32[32]{0:T(128)}, u32[]{:S(2)}) copy-start(s32[32]{0:T(128)} %copy-done.1) | copy-start | bytes 388
  21.7 20.7 %copy-start = (bf16[32,32]{1,0:T(8,128)(2,1)S(1)}, bf16[32,32]{1,0:T(8,128)(2,1)}, u32[]{:S(2)}) copy-start(bf16[32,32]{1,0:T(8,128)(2,1)} %get-tuple-element.19) | copy-start | bytes 6148
  24.4 91.0 %copy-start.4 = (f32[2,2]{0,1:T(2,128)S(1)}, f32[2,2]{0,1:T(2,128)}, u32[]{:S(2)}) copy-start(f32[2,2]{0,1:T(2,128)} %copy-done.3) | copy-start | bytes 52
Sparse Core Ops, SparseCore 0:
  11.0 59.4 all-gather.3
  75.4 57.9 all-gather.5
